TPU v7x, 128 devices: a whole 4x4x4 slice. The times are simulated.
128 devices in a mesh: depth: 2 (over core), rows: 2 (over x_hi), shots: 32 (over z, y, x_lo).
Axes of the slice: x: 4 (x_hi: 2, x_lo: 2; x = x_hi * 2 + x_lo), y: 4, z: 4, core: 2. Of those that a mesh axis runs over, the one named last changes fastest.
Arguments:
- sources: float32 [2, 2, 1024, 4096], P('depth', None, 'rows', 'shots'), may hold values from -6 to 6
- factor: float32 [2, 2, 1024, 1024], P('depth', None, ('rows', 'shots')), may hold values from -0.09375 to 0.09375
- block_mask: int32 [2, 2, 8, 8], P('depth'), may hold values 0 or 1
- inverse_diagonal: float32 [2, 2, 1024, 1024], P('depth', None, None, 'rows'), may hold values from -1.2 to 1.2, as said below
Outputs:
- solution: float32 [2, 2, 1024, 4096], P('depth', None, 'rows', 'shots')
Inputs may be any that keep to these rules, and one draw needn't show every extreme that they name: Each block inverse_diagonal[d, m] is lower triangular with diagonal entries between 0.8 and 1.2.
All inputs are finite; a program needn't handle non-finite values. No bound on the sum of `block_mask` on one device may be relied on, other than what follows from the above.
Results may differ from a plain program's by a relative error of at most 0.0001.
Values sent between devices are 32-bit elements; how exact they have to be, the bound alone decides.
A program may use at most 64 MiB of HBM per device.

v0:
```python
import jax
import jax.numpy as jnp
from jax import lax
from jax.sharding import PartitionSpec as P


def mask_rows(factor_rows, block_mask, row_start, block_size):
    row_total = factor_rows.shape[1]
    block_count = block_mask.shape[3]
    row_blocks = (row_start + jnp.arange(row_total, dtype=jnp.int32)) // block_size
    row_select = (row_blocks[:, None] == jnp.arange(block_count, dtype=jnp.int32)[None, :]).astype(
        jnp.float32
    )
    row_masks = jnp.einsum("rk,pkc->prc", row_select, block_mask[0].astype(jnp.float32))
    return factor_rows * jnp.repeat(row_masks, block_size, axis=2)


def group_reduce(partial_value):
    summed = lax.psum_scatter(partial_value, "depth", scatter_dimension=0, tiled=True)
    return summed[0]


def group_collect(spread):
    every_rows = lax.all_gather(spread[None], "depth", axis=0, tiled=True)
    return every_rows


def invert_level(inverse_block, own_rows):
    inverse_term = jnp.dot(
        inverse_block, own_rows, precision=lax.Precision.HIGHEST, preferred_element_type=jnp.float32
    )
    return lax.psum(inverse_term, "rows")


def per_device(sources, factor, block_mask, inverse_diagonal):
    depth_count = lax.axis_size("depth")
    tree_height = depth_count.bit_length() - 1
    level_count = tree_height + 1
    shot_index = lax.axis_index("shots")
    rows_index = lax.axis_index("rows")
    thin_rows = factor.shape[2]
    full_width = factor.shape[3]
    block_count = block_mask.shape[3]
    block_size = full_width // block_count
    highest = lax.Precision.HIGHEST
    row_start = (rows_index * lax.axis_size("shots") + shot_index) * thin_rows
    masked = mask_rows(factor[0], block_mask, row_start, block_size)
    solved = []
    wide_solved = []
    for tier_index in range(level_count):
        own_rows = sources[0, tier_index]
        if tier_index > 0:
            group_size = 2**tier_index
            factor_tiles = masked.reshape(tier_index, group_size, thin_rows, full_width)
            lower_solved = jnp.stack(wide_solved[:tier_index])
            partial_value = jnp.einsum(
                "lgrs,lsn->grn",
                factor_tiles,
                lower_solved,
                precision=highest,
                preferred_element_type=jnp.float32,
            )
            reduced = group_reduce(partial_value)
            reduced = lax.all_to_all(reduced, "shots", split_axis=1, concat_axis=0, tiled=True)
            own_rows = own_rows - reduced
        full_rows = invert_level(inverse_diagonal[0, tier_index], own_rows)
        solved.append(full_rows)
        if tier_index < tree_height:
            wide_solved.append(lax.all_gather(full_rows, "shots", axis=1, tiled=True))
    answers = [None] * level_count
    collected = {}
    for tier_index in reversed(range(level_count)):
        target = solved[tier_index]
        if tier_index < tree_height:
            factor_tiles = masked
            transposed = jnp.einsum(
                "grs,grn->sn",
                factor_tiles,
                collected[1],
                precision=highest,
                preferred_element_type=jnp.float32,
            )
            shot_piece = lax.psum_scatter(transposed, "shots", scatter_dimension=1, tiled=True)
            own_columns = lax.psum(shot_piece, "rows")
            target = target - own_columns
        answer = lax.dot_general(
            inverse_diagonal[0, tier_index],
            target,
            (((0,), (0,)), ((), ())),
            precision=highest,
            preferred_element_type=jnp.float32,
        )
        answers[tier_index] = answer
        if tier_index > 0:
            spread = lax.all_to_all(answer, "shots", split_axis=0, concat_axis=1, tiled=True)
            collected[tier_index] = group_collect(spread)
    return jnp.stack(answers)[None]


def solution(mesh):
    placed = (
        P("depth", None, "rows", "shots"),
        P("depth", None, ("rows", "shots"), None),
        P("depth", None, None, None),
        P("depth", None, None, "rows"),
    )
    return jax.shard_map(
        per_device,
        mesh=mesh,
        in_specs=placed,
        out_specs=P("depth", None, "rows", "shots"),
        check_vma=False,
    )
```

profile of v0, /device:TPU:1, one launch (start us, length us, event | category | flops | bytes accessed | tf_op | source)
XLA Modules:
  0.0 942.0 jit_solution(3403991604582665466)
XLA Ops:
  6.5 0.0 copy-start.1
  6.5 0.0 all-reduce.4.cloned.1.call-start
  6.5 4.2 fusion.8
  10.8 0.0 all-reduce.4.cloned.1.call-update
  10.8 0.0 all-gather.2.cloned.1.call-start
  10.8 40.0 %all-reduce.4.cloned.1.call-done = f32[1024,128]{1,0:T(8,128)} async-done(((f32[1024,128]{1,0:T(8,128)}), f32[1024,128]{1,0:T(8,128)}) %all-reduce.4.cloned.1.call-update) | async-done | bytes 524304 | tf_op jit(solution)/shard_map/psum | solution.py:32
  50.8 0.0 all-gather.2.cloned.1.call-update
  50.8 0.0 reduce-scatter.3.cloned.1.call-start
  50.9 0.7 convert_bitcast_fusion
  51.6 0.1 copy.15
  51.7 0.1 convolution_bitcast_fusion.1
  51.8 0.1 copy.16
  51.9 0.1 broadcast_in_dim.11
  52.0 0.0 copy-start.2
  52.0 359.2 %all-gather.2.cloned.1.call-done = f32[1024,4096]{1,0:T(8,128)} async-done(((f32[1024,128]{1,0:T(8,128)}), f32[1024,4096]{1,0:T(8,128)}) %all-gather.2.cloned.1.call-update) | async-done | bytes 16777232 | tf_op jit(solution)/shard_map/all_gather | solution.py:69
  411.2 0.0 copy-done.1
  411.2 13.9 %fusion = f32[2,16,4096]{2,1,0:T(8,128)} fusion(f32[1024,4096]{1,0:T(8,128)} %all-gather.2.cloned.1.call-done, f32[1,2,16,1024]{3,2,1,0:T(8,128)S(1)} %copy-done.1, f32[1,2,16,1024]{3,2,1,0:T(8,128)S(1)} %reshape.43), kind=kOutput, calls=%fused_computation | convolution fusion | flops 1610645504 | bytes 17563648 | tf_op jit(solution)/shard_map/lgrs,lsn->grn/dot_general | solution.py:56
  425.1 0.0 reduce-scatter.3.cloned.1.call-update
  425.2 0.0 all-reduce.6.cloned.1.call-start
  425.2 12.2 %reduce-scatter.3.cloned.1.call-done = f32[1,16,4096]{2,1,0:T(8,128)} async-done(((f32[2,16,4096]{2,1,0:T(8,128)}), f32[1,16,4096]{2,1,0:T(8,128)}) %reduce-scatter.3.cloned.1.call-update) | async-done | bytes 262160 | tf_op jit(solution)/shard_map/reduce_scatter | solution.py:19
  437.4 1.0 copy.21
  438.4 0.2 copy.17
  438.6 16.8 %all_to_all.35 = f32[16,32,128]{2,0,1:T(8,128)S(1)} all-to-all(f32[16,32,128]{2,0,1:T(8,128)S(1)} %copy.17), channel_id=1, replica_groups=mesh['depth'=2,'rows'=2,'shots'=32] {'shots'}, dimensions={1} | all-to-all | bytes 524288 | tf_op jit(solution)/shard_map/all_to_all | solution.py:64
  455.4 0.0 copy-done.2
  455.4 4.7 fusion.14
  460.1 0.0 all-reduce.6.cloned.1.call-update
  460.1 34.9 %all-reduce.6.cloned.1.call-done = f32[1024,128]{0,1:T(8,128)} async-done(((f32[1024,128]{0,1:T(8,128)}), f32[1024,128]{0,1:T(8,128)}) %all-reduce.6.cloned.1.call-update) | async-done | bytes 524304 | tf_op jit(solution)/shard_map/psum | solution.py:32
  494.9 3.1 fusion.2
  498.0 0.8 copy.18
  498.8 7.0 all-to-all-start.1
  505.8 0.0 reduce-scatter.5.cloned.1.call-start
  505.9 8.5 all-to-all-done.1
  514.4 0.1 copy.19
  514.5 0.1 broadcast_in_dim.12
  514.6 3.8 all_gather.7
  518.4 16.0 %convolution_bitcast_fusion = f32[1024,4096]{1,0:T(8,128)} fusion(f32[2,16,4096]{2,1,0:T(8,128)S(1)} %all_gather.7, f32[2,16,1024]{2,1,0:T(8,128)S(1)} %reshape.42, f32[1,2,16,1024]{3,2,1,0:T(8,128)S(1)} %copy-done.1), kind=kOutput, calls=%fused_computation.2 | convolution fusion | flops 1610645504 | bytes 17563648 | tf_op jit(solution)/shard_map/grs,grn->sn/dot_general | solution.py:76
  534.3 0.0 copy-start
  534.3 0.0 reduce-scatter.5.cloned.1.call-update
  534.3 0.0 all-reduce.8.cloned.1.call-start
  534.4 359.6 %reduce-scatter.5.cloned.1.call-done = f32[1024,128]{1,0:T(8,128)} async-done(((f32[1024,4096]{1,0:T(8,128)}), f32[1024,128]{1,0:T(8,128)}) %reduce-scatter.5.cloned.1.call-update) | async-done | bytes 524304 | tf_op jit(solution)/shard_map/reduce_scatter | solution.py:83
  894.0 0.0 all-reduce.8.cloned.1.call-update
  894.0 36.9 %all-reduce.8.cloned.1.call-done = f32[1024,128]{1,0:T(8,128)} async-done(((f32[1024,128]{1,0:T(8,128)}), f32[1024,128]{1,0:T(8,128)}) %all-reduce.8.cloned.1.call-update) | async-done | bytes 524304 | tf_op jit(solution)/shard_map/psum | solution.py:84
  930.9 0.0 copy-done
  930.9 3.2 fusion.17
  934.1 1.0 copy.20
  (4 shorter events, 0.1 us)
Async XLA Ops:
  6.5 404.7 %copy-start.1 = (f32[1,2,16,1024]{3,2,1,0:T(8,128)S(1)}, f32[1,2,16,1024]{3,2,1,0:T(8,128)}, u32[]{:S(2)}) copy-start(f32[1,2,16,1024]{3,2,1,0:T(8,128)} %param.5) | copy-start | bytes 393220
  6.5 44.3 %all-reduce.4.cloned.1.call-start = ((), (), s32[]{:S(2)}) async-start(), calls=%async_computation.4 | async-start | bytes 1048576 | tf_op jit(solution)/shard_map/psum | solution.py:32
  10.8 400.5 %all-gather.2.cloned.1.call-start = ((), (), s32[]{:S(2)}) async-start(), calls=%async_computation.5 | async-start | bytes 17301504 | tf_op jit(solution)/shard_map/all_gather | solution.py:69
  50.8 386.6 %reduce-scatter.3.cloned.1.call-start = ((), (), s32[]{:S(2)}) async-start(), calls=%async_computation.6 | async-start | bytes 786432 | tf_op jit(solution)/shard_map/reduce_scatter | solution.py:19
  52.0 403.4 %copy-start.2 = (f32[1,2,512,128]{3,2,1,0:T(8,128)S(1)}, f32[1,2,512,128]{3,2,1,0:T(8,128)}, u32[]{:S(2)}) copy-start(f32[1,2,512,128]{3,2,1,0:T(8,128)} %param.4) | copy-start | bytes 1572868
  425.2 69.8 %all-reduce.6.cloned.1.call-start = ((), (), s32[]{:S(2)}) async-start(), calls=%async_computation.7 | async-start | bytes 1048576 | tf_op jit(solution)/shard_map/psum | solution.py:32
  498.8 15.6 %all-to-all-start.1 = ((f32[32,16,128]{2,1,0:T(8,128)}), f32[32,16,128]{2,1,0:T(8,128)S(1)}, u32[]{:S(2)}, u32[]{:S(2)}) async-start(f32[32,16,128]{2,1,0:T(8,128)} %bitcast.16), calls=%async_computation.2 | async-start | bytes 524288 | tf_op jit(solution)/shard_map/all_to_all | solution.py:95
  505.8 388.2 %reduce-scatter.5.cloned.1.call-start = ((), (), s32[]{:S(2)}) async-start(), calls=%async_computation.8 | async-start | bytes 17301504 | tf_op jit(solution)/shard_map/reduce_scatter | solution.py:83
  534.3 396.6 %copy-start = (f32[1024,128]{1,0:T(8,128)S(1)}, f32[1024,128]{1,0:T(8,128)}, u32[]{:S(2)}) copy-start(f32[1024,128]{1,0:T(8,128)} %all-reduce.4.cloned.1.call-done) | copy-start | bytes 1572868
  534.3 396.6 %all-reduce.8.cloned.1.call-start = ((), (), s32[]{:S(2)}) async-start(), calls=%async_computation.9 | async-start | bytes 1048576 | tf_op jit(solution)/shard_map/psum | solution.py:84
Sparse Core Ops, SparseCore 0:
  10.9 39.8 all-reduce.3
  52.5 358.7 all-gather.1
  425.3 12.0 reduce-scatter.2
  460.2 34.6 all-reduce.5
  534.5 359.4 reduce-scatter.4
  896.5 34.4 all-reduce.7
where the time goes:
time: 942 us
  waiting for transfers between devices  851 us (90%)
  matrix products  45.1 us (5%)
  blocking collectives  20.6 us (2%)
  between operations  13.6 us (1%)
    reduce_scatter x1, waiting for transfers between devices, per_device(): lax.psum_scatter(transposed, 'shots', scatter_dimension=1, tiled=True)  360 us
    all_gather x1, waiting for transfers between devices, per_device(): wide_solved.append(lax.all_gather(full_rows, 'shots', axis=1, tiled=True))  359 us
    psum x2, waiting for transfers between devices, invert_level(): return lax.psum(inverse_term, 'rows')  74.8 us
    psum x1, waiting for transfers between devices, per_device(): own_columns = lax.psum(shot_piece, 'rows')  36.9 us
  transfers between devices with their start and end apart: 7, of which 7 were waited for; matrix products, arithmetic and copies ran while one was open for 0% of the time, Pallas kernels for 0%

commit v1 on v0

--- a/solution.py
+++ b/solution.py
@@ -81,7 +81,8 @@
                 preferred_element_type=jnp.float32,
             )
             shot_piece = lax.psum_scatter(transposed, "shots", scatter_dimension=1, tiled=True)
-            own_columns = lax.psum(shot_piece, "rows")
+            parts = lax.all_gather(shot_piece, "rows", axis=0, tiled=False)
+            own_columns = parts.sum(axis=0)
             target = target - own_columns
         answer = lax.dot_general(
             inverse_diagonal[0, tier_index],

time: 942 us -> 931 us (0.988)
  waiting for transfers between devices: 851 us -> 839 us
    psum x1 -> x0, waiting for transfers between devices: 36.9 us -> none  [per_device(): own_columns = lax.psum(shot_piece, 'rows')]
    all_gather x0 -> x1, waiting for transfers between devices: none -> 24.7 us  [per_device(): parts = lax.all_gather(shot_piece, 'rows', axis=0, tiled=False)]
where the time goes in v1:
time: 931 us
  waiting for transfers between devices  839 us (90%)
  matrix products  44.9 us (5%)
  blocking collectives  20.6 us (2%)
  between operations  13.6 us (1%)
    reduce_scatter x1, waiting for transfers between devices, per_device(): lax.psum_scatter(transposed, 'shots', scatter_dimension=1, tiled=True)  360 us
    all_gather x1, waiting for transfers between devices, per_device(): wide_solved.append(lax.all_gather(full_rows, 'shots', axis=1, tiled=True))  359 us
    psum x2, waiting for transfers between devices, invert_level(): return lax.psum(inverse_term, 'rows')  74.8 us
    all_gather x1, waiting for transfers between devices, per_device(): parts = lax.all_gather(shot_piece, 'rows', axis=0, tiled=False)  24.7 us
  transfers between devices with their start and end apart: 7, of which 7 were waited for; matrix products, arithmetic and copies ran while one was open for 0% of the time, Pallas kernels for 0%

profile of v1, /device:TPU:1, one launch (start us, length us, event | category | flops | bytes accessed | tf_op | source)
XLA Modules:
  0.0 931.0 jit_solution(8326248717552514967)
XLA Ops:
  6.5 0.0 copy-start.1
  6.5 0.0 all-reduce.3.cloned.1.call-start
  6.5 4.2 fusion.8
  10.8 0.0 all-reduce.3.cloned.1.call-update
  10.8 0.0 all-gather.4.cloned.1.call-start
  10.8 40.0 %all-reduce.3.cloned.1.call-done = f32[1024,128]{1,0:T(8,128)} async-done(((f32[1024,128]{1,0:T(8,128)}), f32[1024,128]{1,0:T(8,128)}) %all-reduce.3.cloned.1.call-update) | async-done | bytes 524304 | tf_op jit(solution)/shard_map/psum | solution.py:32
  50.8 0.0 all-gather.4.cloned.1.call-update
  50.8 0.0 reduce-scatter.3.cloned.1.call-start
  50.9 0.7 convert_bitcast_fusion
  51.6 0.1 copy.21
  51.7 0.1 convolution_bitcast_fusion.1
  51.8 0.1 copy.22
  51.9 0.1 broadcast_in_dim.11
  52.0 0.0 copy-start.2
  52.0 359.2 %all-gather.4.cloned.1.call-done = f32[1024,4096]{1,0:T(8,128)} async-done(((f32[1024,128]{1,0:T(8,128)}), f32[1024,4096]{1,0:T(8,128)}) %all-gather.4.cloned.1.call-update) | async-done | bytes 16777232 | tf_op jit(solution)/shard_map/all_gather | solution.py:69
  411.2 0.0 copy-done.1
  411.2 13.9 %fusion = f32[2,16,4096]{2,1,0:T(8,128)} fusion(f32[1024,4096]{1,0:T(8,128)} %all-gather.4.cloned.1.call-done, f32[1,2,16,1024]{3,2,1,0:T(8,128)S(1)} %copy-done.1, f32[1,2,16,1024]{3,2,1,0:T(8,128)S(1)} %reshape.43), kind=kOutput, calls=%fused_computation | convolution fusion | flops 1610645504 | bytes 17563648 | tf_op jit(solution)/shard_map/lgrs,lsn->grn/dot_general | solution.py:56
  425.1 0.0 reduce-scatter.3.cloned.1.call-update
  425.2 0.0 all-reduce.5.cloned.1.call-start
  425.2 12.2 %reduce-scatter.3.cloned.1.call-done = f32[1,16,4096]{2,1,0:T(8,128)} async-done(((f32[2,16,4096]{2,1,0:T(8,128)}), f32[1,16,4096]{2,1,0:T(8,128)}) %reduce-scatter.3.cloned.1.call-update) | async-done | bytes 262160 | tf_op jit(solution)/shard_map/reduce_scatter | solution.py:19
  437.4 1.0 copy.27
  438.4 0.2 copy.23
  438.6 16.8 %all_to_all.35 = f32[16,32,128]{2,0,1:T(8,128)S(1)} all-to-all(f32[16,32,128]{2,0,1:T(8,128)S(1)} %copy.23), channel_id=1, replica_groups=mesh['depth'=2,'rows'=2,'shots'=32] {'shots'}, dimensions={1} | all-to-all | bytes 524288 | tf_op jit(solution)/shard_map/all_to_all | solution.py:64
  455.4 0.0 copy-done.2
  455.4 4.7 fusion.14
  460.1 0.0 all-reduce.5.cloned.1.call-update
  460.1 34.9 %all-reduce.5.cloned.1.call-done = f32[1024,128]{0,1:T(8,128)} async-done(((f32[1024,128]{0,1:T(8,128)}), f32[1024,128]{0,1:T(8,128)}) %all-reduce.5.cloned.1.call-update) | async-done | bytes 524304 | tf_op jit(solution)/shard_map/psum | solution.py:32
  494.9 3.1 fusion.2
  498.0 0.8 copy.24
  498.8 7.0 all-to-all-start.1
  505.8 0.0 reduce-scatter.5.cloned.1.call-start
  505.9 8.5 all-to-all-done.1
  514.4 0.1 copy.25
  514.5 0.1 broadcast_in_dim.12
  514.6 3.8 all_gather.13
  518.4 16.0 %convolution_bitcast_fusion = f32[1024,4096]{1,0:T(8,128)} fusion(f32[2,16,4096]{2,1,0:T(8,128)S(1)} %all_gather.13, f32[2,16,1024]{2,1,0:T(8,128)S(1)} %reshape.42, f32[1,2,16,1024]{3,2,1,0:T(8,128)S(1)} %copy-done.1), kind=kOutput, calls=%fused_computation.2 | convolution fusion | flops 1610645504 | bytes 17563648 | tf_op jit(solution)/shard_map/grs,grn->sn/dot_general | solution.py:76
  534.3 0.0 copy-start
  534.3 0.0 reduce-scatter.5.cloned.1.call-update
  534.3 0.0 all-gather.6.cloned.1.call-start
  534.4 359.6 %reduce-scatter.5.cloned.1.call-done = f32[1024,128]{1,0:T(8,128)} async-done(((f32[1024,4096]{1,0:T(8,128)}), f32[1024,128]{1,0:T(8,128)}) %reduce-scatter.5.cloned.1.call-update) | async-done | bytes 524304 | tf_op jit(solution)/shard_map/reduce_scatter | solution.py:83
  894.0 0.0 all-gather.6.cloned.1.call-update
  894.0 24.7 %all-gather.6.cloned.1.call-done = f32[2048,128]{1,0:T(8,128)} async-done(((f32[1024,128]{1,0:T(8,128)}), f32[2048,128]{1,0:T(8,128)}) %all-gather.6.cloned.1.call-update) | async-done | bytes 1048592 | tf_op jit(solution)/shard_map/all_gather | solution.py:84
  918.7 1.3 reduce_sum.9
  920.1 0.0 copy-done
  920.1 3.0 fusion.17
  923.1 1.0 copy.26
  (4 shorter events, 0.1 us)
Async XLA Ops:
  6.5 404.7 %copy-start.1 = (f32[1,2,16,1024]{3,2,1,0:T(8,128)S(1)}, f32[1,2,16,1024]{3,2,1,0:T(8,128)}, u32[]{:S(2)}) copy-start(f32[1,2,16,1024]{3,2,1,0:T(8,128)} %param.5) | copy-start | bytes 393220
  6.5 44.3 %all-reduce.3.cloned.1.call-start = ((), (), s32[]{:S(2)}) async-start(), calls=%async_computation.4 | async-start | bytes 1048576 | tf_op jit(solution)/shard_map/psum | solution.py:32
  10.8 400.5 %all-gather.4.cloned.1.call-start = ((), (), s32[]{:S(2)}) async-start(), calls=%async_computation.5 | async-start | bytes 17301504 | tf_op jit(solution)/shard_map/all_gather | solution.py:69
  50.8 386.6 %reduce-scatter.3.cloned.1.call-start = ((), (), s32[]{:S(2)}) async-start(), calls=%async_computation.6 | async-start | bytes 786432 | tf_op jit(solution)/shard_map/reduce_scatter | solution.py:19
  52.0 403.4 %copy-start.2 = (f32[1,2,512,128]{3,2,1,0:T(8,128)S(1)}, f32[1,2,512,128]{3,2,1,0:T(8,128)}, u32[]{:S(2)}) copy-start(f32[1,2,512,128]{3,2,1,0:T(8,128)} %param.4) | copy-start | bytes 1572868
  425.2 69.8 %all-reduce.5.cloned.1.call-start = ((), (), s32[]{:S(2)}) async-start(), calls=%async_computation.7 | async-start | bytes 1048576 | tf_op jit(solution)/shard_map/psum | solution.py:32
  498.8 15.6 %all-to-all-start.1 = ((f32[32,16,128]{2,1,0:T(8,128)}), f32[32,16,128]{2,1,0:T(8,128)S(1)}, u32[]{:S(2)}, u32[]{:S(2)}) async-start(f32[32,16,128]{2,1,0:T(8,128)} %bitcast.16), calls=%async_computation.2 | async-start | bytes 524288 | tf_op jit(solution)/shard_map/all_to_all | solution.py:96
  505.8 388.2 %reduce-scatter.5.cloned.1.call-start = ((), (), s32[]{:S(2)}) async-start(), calls=%async_computation.8 | async-start | bytes 17301504 | tf_op jit(solution)/shard_map/reduce_scatter | solution.py:83
  534.3 385.8 %copy-start = (f32[1024,128]{1,0:T(8,128)S(1)}, f32[1024,128]{1,0:T(8,128)}, u32[]{:S(2)}) copy-start(f32[1024,128]{1,0:T(8,128)} %all-reduce.3.cloned.1.call-done) | copy-start | bytes 1572868
  534.3 384.4 %all-gather.6.cloned.1.call-start = ((), (), s32[]{:S(2)}) async-start(), calls=%async_computation.9 | async-start | bytes 1572864 | tf_op jit(solution)/shard_map/all_gather | solution.py:84
Sparse Core Ops, SparseCore 0:
  10.9 39.8 all-reduce.2
  52.5 358.7 all-gather.3
  425.3 12.0 reduce-scatter.2
  460.2 34.6 all-reduce.4
  534.5 359.4 reduce-scatter.4
  895.6 23.0 all-gather.5
